TPU v7x, 512 devices: a whole 4x8x8 slice. The times are simulated.
512 devices in a mesh: space: 128 (over y, z, core), head: 4 (over x).
Axes of the slice: x: 4, y: 8, z: 8, core: 2. Of those that a mesh axis runs over, the one named last changes fastest.
Arguments:
- tokens: bfloat16 [131072, 1024], P('space', 'head'), may hold values from -6 to 6
- norm_gain: float32 [1024], replicated, may hold values from 0.25 to 1.75
- w_qkv: bfloat16 [3, 1024, 1024], P(None, None, 'head'), may hold values from -0.1875 to 0.1875
- w_out: bfloat16 [1024, 1024], P('head'), may hold values from -1 to 1
- window_id: int32 [128, 1024], P('space'), may hold values from 0 to 2, never falling along the last dimension, each value on 1 to 512 neighbouring positions
- carry: int32 [128], P('space'), may hold values from 0 to 256, as said below
Outputs:
- updated: bfloat16 [131072, 1024], P('space', 'head')
Inputs may be any that keep to these rules, and one draw needn't show every extreme that they name: `carry`: the last device carries 0; some other device carries exactly 256. `window_id`: on each device labels never fall along the tokens, each of the 3 labels is used, and some window has exactly 512 tokens.
All inputs are finite; a program needn't handle non-finite values.
Results may differ from a plain program's by a relative error of at most 0.018.
Values may be sent and summed in bfloat16 or wider, within the bound.
A program may use at most 64 MiB of HBM per device.

v0:
```python
import jax
import jax.numpy as jnp
from jax import lax
from jax.sharding import PartitionSpec as P

HS = 64
CAP = 256


eps = 1e-05


def shifted(block, axis, distance):
    devices = range(lax.axis_size(axis))
    route = [(i - distance, i) for i in devices if i - distance in devices]
    return lax.ppermute(block, axis, route)


def attend_block(query, query_lab, kv_rows, key_lab, heads_dev, head_size):
    width = heads_dev * head_size
    key_rows = kv_rows[:, :width].reshape(kv_rows.shape[0], heads_dev, head_size)
    value_rows = kv_rows[:, width:].reshape(kv_rows.shape[0], heads_dev, head_size)
    rows = query.shape[0]
    rows = query.shape[0]
    shaped = query.reshape(rows, heads_dev, head_size)
    scores = jnp.einsum(
        "qhd,khd->hqk", shaped, key_rows, preferred_element_type=jnp.float32
    ) * head_size ** (-0.5)
    allowed = (query_lab[:, None] == key_lab[None, :]) & (query_lab[:, None] >= 0)
    scores = jnp.where(allowed[None], scores, -1e30)
    probs = jax.nn.softmax(scores, axis=-1).astype(jnp.bfloat16)
    out = jnp.einsum("hqk,khd->qhd", probs, value_rows, preferred_element_type=jnp.float32)
    return out.reshape(rows, width).astype(jnp.bfloat16)


def local(tokens, norm_gain, w_qkv, w_out, window_id, carry):
    tok_rows = tokens.shape[0]
    width = w_qkv.shape[2]
    heads_dev = width // HS
    full = lax.all_gather(tokens, "head", axis=1, tiled=True).astype(jnp.float32)
    mean = jnp.mean(full, axis=1, keepdims=True)
    var = jnp.mean((full - mean) ** 2, axis=1, keepdims=True)
    normed = ((full - mean) * lax.rsqrt(var + eps) * norm_gain).astype(jnp.bfloat16)
    qkv = jnp.einsum("td,cde->tce", normed, w_qkv, preferred_element_type=jnp.float32).astype(
        jnp.bfloat16
    )
    qkv = qkv.reshape(tok_rows, 3 * width)
    labels_here = window_id.reshape(tok_rows)
    count = carry[0]
    position = jnp.arange(tok_rows, dtype=jnp.int32)
    moved = position >= tok_rows - count
    tail_code = jnp.where(jnp.arange(CAP, dtype=jnp.int32) >= CAP - count, 1, 0).astype(jnp.int32)
    local_lab = jnp.where(moved, -1, labels_here)
    incoming, incoming_code = shifted((qkv[tok_rows - CAP :], tail_code), "space", 1)
    incoming_lab = (incoming_code - 1).astype(jnp.int32)
    kv_rows = jnp.concatenate([qkv[:, width:], incoming[:, width:]], axis=0)
    key_lab = jnp.concatenate([local_lab, incoming_lab], axis=0)
    own = attend_block(qkv[:, :width], local_lab, kv_rows, key_lab, heads_dev, HS)
    carried = attend_block(incoming[:, :width], incoming_lab, kv_rows, key_lab, heads_dev, HS)
    back = shifted(carried, "space", -1)
    padded = jnp.concatenate([jnp.zeros((tok_rows - CAP, width), jnp.bfloat16), back], axis=0)
    attended = jnp.where(moved[:, None], padded, own)
    residual = tokens.astype(jnp.float32)
    partial_out = jnp.dot(attended, w_out, preferred_element_type=jnp.float32)
    branch = lax.psum_scatter(
        partial_out.astype(jnp.bfloat16), "head", scatter_dimension=1, tiled=True
    ).astype(jnp.float32)
    return (residual + branch).astype(jnp.bfloat16)


def solution(mesh):
    return jax.shard_map(
        local,
        mesh=mesh,
        in_specs=(
            P("space", "head"),
            P(),
            P(None, None, "head"),
            P("head", None),
            P("space", None),
            P("space"),
        ),
        out_specs=P("space", "head"),
        check_vma=False,
    )
```

profile of v0, /device:TPU:1, one launch (start us, length us, event | category | flops | bytes accessed | tf_op | source)
XLA Modules:
  0.0 149.6 jit_solution(10393227315789359971)
XLA Ops:
  6.5 0.0 copy-start
  6.5 0.0 all-gather.2.cloned.1.call-start
  6.5 0.7 all-gather.2.cloned.1.call-update
  7.3 0.0 reduce-scatter.2.cloned.1.call-start
  8.0 5.4 %collective-permute-start.1 = (s32[256]{0:T(256)S(1)}, s32[256]{0:T(256)S(1)}, u32[]{:S(2)}, u32[]{:S(2)}) collective-permute-start(s32[256]{0:T(256)S(1)} %compare_select_fusion), channel_id=1, source_target_pairs={{0,4},{4,8},{8,12},{12,16},{16,20},{20,24},{24,28},{28,32},{32,36}... | collective-permute-start | bytes 3080 | tf_op jit(solution)/shard_map/ppermute | solution.py:16
  13.4 0.7 broadcast_compare_fusion
  14.1 2.7 %collective-permute-done.1 = s32[256]{0:T(256)S(1)} collective-permute-done((s32[256]{0:T(256)S(1)}, s32[256]{0:T(256)S(1)}, u32[]{:S(2)}, u32[]{:S(2)}) %collective-permute-start.1) | collective-permute-done | bytes 1056 | tf_op jit(solution)/shard_map/ppermute | solution.py:16
  16.8 1.2 compare_and_fusion
  18.0 0.0 copy-start.3
  18.0 35.9 %all-gather.2.cloned.1.call-done = bf16[1024,1024]{1,0:T(8,128)(2,1)} async-done(((bf16[1024,256]{1,0:T(8,128)(2,1)}), bf16[1024,1024]{1,0:T(8,128)(2,1)}) %all-gather.2.cloned.1.call-update) | async-done | bytes 2097168 | tf_op jit(solution)/shard_map/all_gather | solution.py:40
  53.9 0.0 copy-start.1
  53.9 2.1 %convert_reduce_fusion = f32[1024]{0:T(1024)S(1)} fusion(bf16[1024,1024]{1,0:T(8,128)(2,1)} %all-gather.2.cloned.1.call-done), kind=kLoop, calls=%fused_computation.9 | loop fusion | flops 2096128 | bytes 2101248 | tf_op jit(solution)/shard_map/reduce_sum | solution.py:41
  56.0 0.1 copy-done.1
  56.1 0.7 fusion.8
  56.8 0.0 copy-done
  56.9 0.0 copy-done.3
  56.9 2.1 %fusion.21 = bf16[1024,3,256]{0,2,1:T(8,128)(2,1)S(1)} fusion(bf16[3,1024,256]{2,1,0:T(8,128)(2,1)S(1)} %copy-done, bf16[1024,1024]{1,0:T(8,128)(2,1)S(1)} %copy-done.1, f32[1024]{0:T(1024)S(1)} %copy-done.3, f32[1024]{0:T(1024)S(1)} %add_rsqrt_fusion, f32[1024]{0:T(1024)S(1)} %broadcast_multiply_fusion), kind=kOutput, calls=%fused_computation.30 | convolution fusion | flops 1616642048 | bytes 5255168 | tf_op jit(solution)/shard_map/td,cde->tce/dot_general | solution.py:44
  59.0 0.1 slice.35
  59.1 4.7 %collective-permute-start = (bf16[256,768]{0,1:T(8,128)(2,1)S(1)}, bf16[256,768]{0,1:T(8,128)(2,1)S(1)}, u32[]{:S(2)}, u32[]{:S(2)}) collective-permute-start(bf16[256,768]{0,1:T(8,128)(2,1)S(1)} %bitcast.44), channel_id=1, source_target_pairs={{0,4},{4,8},{8,12},{12,16},{16,20},{20,24},{24,28},{28,32},{32,36}... | collective-permute-start | bytes 1179656 | tf_op jit(solution)/shard_map/ppermute | solution.py:16
  63.8 1.0 compare_and_fusion.1
  64.8 0.8 slice.40
  65.6 0.1 slice.34
  65.7 2.8 %collective-permute-done = bf16[256,768]{0,1:T(8,128)(2,1)S(1)} collective-permute-done((bf16[256,768]{0,1:T(8,128)(2,1)S(1)}, bf16[256,768]{0,1:T(8,128)(2,1)S(1)}, u32[]{:S(2)}, u32[]{:S(2)}) %collective-permute-start) | collective-permute-done | bytes 393248 | tf_op jit(solution)/shard_map/ppermute | solution.py:16
  68.5 0.9 pad_maximum_fusion
  69.4 0.7 slice.39
  70.1 3.0 %exponential_reduce_fusion.1 = f32[4,256]{1,0:T(4,128)S(1)} fusion(pred[256,1280]{1,0:T(8,128)(4,1)} %compare_and_fusion.1, bf16[256,4,64]{0,2,1:T(8,128)(2,1)} %bitcast.45, bf16[1280,4,64]{0,2,1:T(8,128)(2,1)S(1)} %bitcast.36), kind=kOutput, calls=%fused_computation.15 | convolution fusion | flops 173016320 | bytes 1118208 | tf_op jit(solution)/shard_map/sub | solution.py:31
  73.1 4.0 %fusion.25 = bf16[4,64,256]{2,1,0:T(8,128)(2,1)} fusion(bf16[1280,4,64]{0,2,1:T(8,128)(2,1)} %bitcast.40, f32[4,256]{1,0:T(4,128)S(1)} %exponential_reduce_fusion.1, pred[256,1280]{1,0:T(8,128)(4,1)} %compare_and_fusion.1, bf16[256,4,64]{0,2,1:T(8,128)(2,1)} %bitcast.46, bf16[1280,4,64]{0,2,1:T(8,128)(2,1)S(1)} %bitcast.37), kind=kOutput, calls=%fused_computation.35 | convolution fusion | flops 342165760 | bytes 1904640 | tf_op jit(solution)/shard_map/hqk,khd->qhd/dot_general | solution.py:32
  77.1 2.1 %collective-permute-start.2 = (bf16[256,256]{0,1:T(8,128)(2,1)}, bf16[256,256]{0,1:T(8,128)(2,1)}, u32[]{:S(2)}, u32[]{:S(2)}) collective-permute-start(bf16[256,256]{0,1:T(8,128)(2,1)} %bitcast.48), channel_id=1, source_target_pairs={{4,0},{8,4},{12,8},{16,12},{20,16},{24,20},{28,24},{32,28},{36,32}... | collective-permute-start | bytes 393224 | tf_op jit(solution)/shard_map/ppermute | solution.py:16
  79.2 9.0 %exponential_reduce_fusion = f32[4,1024]{1,0:T(4,128)} fusion(bf16[1024,4,64]{0,2,1:T(8,128)(2,1)} %bitcast.42, bf16[1280,4,64]{0,2,1:T(8,128)(2,1)S(1)} %bitcast.38, pred[1024,1280]{1,0:T(8,128)(4,1)S(1)} %compare_and_fusion), kind=kOutput, calls=%fused_computation.5 | convolution fusion | flops 692061440 | bytes 2506752 | tf_op jit(solution)/shard_map/sub | solution.py:31
  88.2 9.9 %fusion.24 = bf16[4,64,1024]{2,1,0:T(8,128)(2,1)} fusion(bf16[1280,4,64]{0,2,1:T(8,128)(2,1)} %bitcast.41, f32[4,1024]{1,0:T(4,128)} %exponential_reduce_fusion, bf16[1024,4,64]{0,2,1:T(8,128)(2,1)} %bitcast.43, bf16[1280,4,64]{0,2,1:T(8,128)(2,1)S(1)} %bitcast.39, pred[1024,1280]{1,0:T(8,128)(4,1)S(1)} %compare_and_fusion), kind=kOutput, calls=%fused_computation.34 | convolution fusion | flops 1368659200 | bytes 3686400 | tf_op jit(solution)/shard_map/hqk,khd->qhd/dot_general | solution.py:32
  98.2 0.0 collective-permute-done.2
  98.2 1.2 bitcast_select_fusion
  99.4 0.0 copy-start.2
  99.4 3.2 %convolution_convert_fusion = bf16[1024,1024]{1,0:T(8,128)(2,1)} fusion(bf16[1024,256]{0,1:T(8,128)(2,1)S(1)} %bitcast_select_fusion, bf16[256,1024]{1,0:T(8,128)(2,1)} %param.9), kind=kOutput, calls=%fused_computation.29 | convolution fusion | flops 537919488 | bytes 3145728 | tf_op jit(solution)/shard_map/dot_general | solution.py:64
  102.6 0.0 reduce-scatter.2.cloned.1.call-update
  102.6 38.2 %reduce-scatter.2.cloned.1.call-done = bf16[1024,256]{1,0:T(8,128)(2,1)} async-done(((bf16[1024,1024]{1,0:T(8,128)(2,1)}), bf16[1024,256]{1,0:T(8,128)(2,1)}) %reduce-scatter.2.cloned.1.call-update) | async-done | bytes 524304 | tf_op jit(solution)/shard_map/reduce_scatter | solution.py:65
  140.8 0.0 copy-done.2
  140.8 2.0 %add_convert_fusion = bf16[1024,256]{1,0:T(8,128)(2,1)} fusion(bf16[1024,256]{1,0:T(8,128)(2,1)} %reduce-scatter.2.cloned.1.call-done, bf16[1024,256]{1,0:T(8,128)(2,1)S(1)} %copy-done.2), kind=kLoop, calls=%fused_computation.36 | loop fusion | flops 1048576 | bytes 1572864 | tf_op jit(solution)/shard_map/convert_element_type | solution.py:68
  (8 shorter events, 0.1 us)
Async XLA Ops:
  6.5 50.3 %copy-start = (bf16[3,1024,256]{2,1,0:T(8,128)(2,1)S(1)}, bf16[3,1024,256]{2,1,0:T(8,128)(2,1)}, u32[]{:S(2)}) copy-start(bf16[3,1024,256]{2,1,0:T(8,128)(2,1)} %param.8) | copy-start | bytes 4718596
  6.5 47.4 %all-gather.2.cloned.1.call-start = ((), (), s32[]{:S(2)}) async-start(), calls=%async_computation.1 | async-start | bytes 2621440 | tf_op jit(solution)/shard_map/all_gather | solution.py:40
  7.3 133.5 %reduce-scatter.2.cloned.1.call-start = ((), (), s32[]{:S(2)}) async-start(), calls=%async_computation.2 | async-start | bytes 2621440 | tf_op jit(solution)/shard_map/reduce_scatter | solution.py:65
  8.0 8.8 %collective-permute-start.1 = (s32[256]{0:T(256)S(1)}, s32[256]{0:T(256)S(1)}, u32[]{:S(2)}, u32[]{:S(2)}) collective-permute-start(s32[256]{0:T(256)S(1)} %compare_select_fusion), channel_id=1, source_target_pairs={{0,4},{4,8},{8,12},{12,16},{16,20},{20,24},{24,28},{28,32},{32,36}... | collective-permute-start | bytes 3080 | tf_op jit(solution)/shard_map/ppermute | solution.py:16
  18.0 38.9 %copy-start.3 = (f32[1024]{0:T(1024)S(1)}, f32[1024]{0:T(1024)}, u32[]{:S(2)}) copy-start(f32[1024]{0:T(1024)} %param.7) | copy-start | bytes 12292
  53.9 2.2 %copy-start.1 = (bf16[1024,1024]{1,0:T(8,128)(2,1)S(1)}, bf16[1024,1024]{1,0:T(8,128)(2,1)}, u32[]{:S(2)}) copy-start(bf16[1024,1024]{1,0:T(8,128)(2,1)} %all-gather.2.cloned.1.call-done) | copy-start | bytes 6291460
  59.1 9.4 %collective-permute-start = (bf16[256,768]{0,1:T(8,128)(2,1)S(1)}, bf16[256,768]{0,1:T(8,128)(2,1)S(1)}, u32[]{:S(2)}, u32[]{:S(2)}) collective-permute-start(bf16[256,768]{0,1:T(8,128)(2,1)S(1)} %bitcast.44), channel_id=1, source_target_pairs={{0,4},{4,8},{8,12},{12,16},{16,20},{20,24},{24,28},{28,32},{32,36}... | collective-permute-start | bytes 1179656 | tf_op jit(solution)/shard_map/ppermute | solution.py:16
  77.1 21.0 %collective-permute-start.2 = (bf16[256,256]{0,1:T(8,128)(2,1)}, bf16[256,256]{0,1:T(8,128)(2,1)}, u32[]{:S(2)}, u32[]{:S(2)}) collective-permute-start(bf16[256,256]{0,1:T(8,128)(2,1)} %bitcast.48), channel_id=1, source_target_pairs={{4,0},{8,4},{12,8},{16,12},{20,16},{24,20},{28,24},{32,28},{36,32}... | collective-permute-start | bytes 393224 | tf_op jit(solution)/shard_map/ppermute | solution.py:16
  99.4 41.4 %copy-start.2 = (bf16[1024,256]{1,0:T(8,128)(2,1)S(1)}, bf16[1024,256]{1,0:T(8,128)(2,1)}, u32[]{:S(2)}) copy-start(bf16[1024,256]{1,0:T(8,128)(2,1)} %param.6) | copy-start | bytes 1572868
Sparse Core Ops, SparseCore 0:
  9.5 44.4 all-gather.1
  102.7 37.9 reduce-scatter.1
where the time goes:
time: 150 us
  waiting for transfers between devices  80.3 us (54%)
  matrix products  31.3 us (21%)
  between operations  14.2 us (9%)
  starting transfers between devices  12.2 us (8%)
  other arithmetic  9.78 us (7%)
  local copies, waits for them, and re-layouts  1.78 us (1%)
    reduce_scatter x1, waiting for transfers between devices, local(): lax.psum_scatter(partial_out.astype(jnp.bfloat16), 'head', scatter_dimens...  38.2 us
    all_gather x1, waiting for transfers between devices, local(): lax.all_gather(tokens, 'head', axis=1, tiled=True).astype(jnp.float32)  35.9 us
    dot_general x2, matrix products, attend_block(): jnp.einsum('hqk,khd->qhd', probs, value_rows, preferred_element_type=jnp....  13.9 us
    ppermute x3, starting transfers between devices, shifted(): return lax.ppermute(block, axis, route)  12.2 us
    sub x2, matrix products, attend_block(): probs = jax.nn.softmax(scores, axis=-1).astype(jnp.bfloat16)  12 us
    ppermute x3, waiting for transfers between devices, shifted(): return lax.ppermute(block, axis, route)  5.47 us
    dot_general x1, matrix products, local(): partial_out = jnp.dot(attended, w_out, preferred_element_type=jnp.float32)  3.2 us
  transfers between devices with their start and end apart: 5, of which 4 were waited for; matrix products, arithmetic and copies ran while one was open for 15% of the time, Pallas kernels for 0%

commit v1 on v0

v1 whole, which is shorter than its diff:
```python
import functools
import math

import jax
import jax.numpy as jnp
from jax import lax
from jax.experimental import pallas as pl
from jax.experimental.pallas import tpu as pltpu
from jax.sharding import PartitionSpec as P

MESH = pl.DeviceIdType.MESH
F32 = jnp.float32
BF16 = jnp.bfloat16

HS = 64
CAP = 256
ROWS = 1024
ALL = ROWS + CAP
WIDTH = 256
PARTS = 4
CH = 128
NCH = ROWS // CH
BLK = 256
NBLK = ROWS // BLK
AHEAD = 3
TILE = 16
EPS = 1e-05
QSCALE = HS**-0.5 * math.log2(math.e)
NEG = -1e30


def chunk_at(i):
    return (i + NCH - CAP // CH) % NCH


def kernel(
    tok_hbm, gain_hbm, wqkv_hbm, wout_hbm, wid_hbm, carry_ref, out_any,
    gain_ref, wid_ref, xg, wq, wo, normed, qk, vv, lab, labin, bias, labcol, back, att, attin, part, hop, relay, fin,
    score, prob, outv,
    own_sem, wsem, ag_send, ag_recv, c_send, c_recv, t_send, t_recv, b_send, b_recv,
    rs_send, rs_recv, out_sem,
):
    me = lax.axis_index("head")
    spot = lax.axis_index("space")
    spots = lax.axis_size("space")
    right, left = lax.rem(me + 1, PARTS), lax.rem(me + PARTS - 1, PARTS)
    far = lax.rem(me + 2, PARTS)
    after, before = lax.rem(spot + 1, spots), lax.rem(spot + spots - 1, spots)
    to_right, to_left = {"head": right}, {"head": left}
    to_after, to_before = {"space": after}, {"space": before}

    own = pltpu.make_async_copy(tok_hbm, xg.at[me], own_sem)
    own.start()

    barrier = pltpu.get_barrier_semaphore()
    for there in (to_right, to_left, to_before):
        pl.semaphore_signal(barrier, inc=1, device_id=there, device_id_type=MESH)

    load_wid = pltpu.make_async_copy(wid_hbm, wid_ref, wsem.at[2])
    load_wid.start()
    load_gain = pltpu.make_async_copy(gain_hbm, gain_ref, wsem.at[3])
    load_gain.start()
    load_wq = pltpu.make_async_copy(wqkv_hbm, wq, wsem.at[0])
    load_wq.start()
    load_wo = pltpu.make_async_copy(wout_hbm, wo, wsem.at[1])
    load_wo.start()

    count = carry_ref[0]
    lab[...] = jnp.full(lab.shape, count, jnp.int32).astype(F32)
    own.wait()
    pl.semaphore_wait(barrier, 3)

    def remote(src, dst, send, recv, there):
        return pltpu.make_async_remote_copy(
            src_ref=src, dst_ref=dst, send_sem=send, recv_sem=recv, device_id=there, device_id_type=MESH
        )

    def gather_copy(kind, i):
        rows = chunk_at(i) * CH
        slot, start, size, there = (
            (me, rows, CH, to_right),
            (me, rows, CH, to_left),
            (left, rows, CH // 2, to_right),
            (right, rows + CH // 2, CH // 2, to_left),
        )[kind]
        view = xg.at[slot, pl.ds(pl.multiple_of(start, CH // 2), size), :]
        return remote(view, view, ag_send.at[kind, i], ag_recv.at[kind, i], there)

    def gather_wait(kind, i):
        rows = chunk_at(i) * CH
        slot, start, size = (
            (left, rows, CH),
            (right, rows, CH),
            (far, rows, CH // 2),
            (far, rows + CH // 2, CH // 2),
        )[kind]
        view = xg.at[slot, pl.ds(pl.multiple_of(start, CH // 2), size), :]
        remote(view, view, ag_send.at[kind, i], ag_recv.at[kind, i], to_right).wait_recv()

    for i in range(AHEAD):
        gather_copy(0, i).start()
        gather_copy(1, i).start()
    code = remote(lab, labin, c_send, c_recv, to_after)
    code.start()

    vv[:, :, CH:] = jnp.ones((2, ALL, CH), BF16)

    def columns_of(queries, first):
        for k in range(queries.shape[1] // CH):
            piece = jnp.broadcast_to(queries[0:1, k * CH : (k + 1) * CH], (CH, CH))
            labcol[first + k * CH : first + (k + 1) * CH, :] = piece.T

    def allow(block, queries, first, start, stop):
        keys = jnp.where(queries < 0.0, -2.0, queries)
        rows = slice(block * BLK, (block + 1) * BLK)
        column = labcol[rows, :]
        for k in range(start, stop, CH):
            bias[rows, k : k + CH] = jnp.where(column == keys[0:1, k - first : k - first + CH], 0.0, NEG)

    def labels_here():
        spread = jnp.broadcast_to(wid_ref[...].astype(F32), (8, ROWS))
        place = lax.broadcasted_iota(jnp.int32, (8, ROWS), 1)
        return jnp.where(place >= ROWS - count, -1.0, spread)

    bands = {0: (0, 768), 1: (0, 1024), 2: (0, 1280), 3: (256, 1024), 4: (512, 768)}
    load_wid.wait()
    mine = labels_here()
    columns_of(mine, CAP)
    for block in range(1, NBLK + 1):
        first, extent = bands[block]
        allow(block, mine, CAP, max(first, CAP), first + extent)

    def admit():
        code.wait_recv()
        place = lax.broadcasted_iota(jnp.int32, (8, CAP), 1).astype(F32)
        theirs = jnp.where(place >= CAP - labin[0:1, 0:1], 0.0, -1.0)
        columns_of(theirs, 0)
        for block in range(3):
            allow(block, theirs, 0, 0, CAP)
        allow(0, labels_here(), CAP, CAP, 768)

    load_gain.wait()
    load_wq.wait()
    gain = gain_ref[...]

    def project(i):
        gather_wait(2, i)
        gather_wait(3, i)
        rows = pl.multiple_of(chunk_at(i) * CH, CH)
        for r in range(0, CH, TILE):
            slices = [
                xg[p, pl.ds(pl.multiple_of(rows + r, TILE), TILE), :].astype(F32) for p in range(PARTS)
            ]
            mean = jnp.sum(sum(slices), axis=1, keepdims=True) * (1.0 / (PARTS * WIDTH))
            centred = [x - mean for x in slices]
            var = jnp.sum(sum(x * x for x in centred), axis=1, keepdims=True) * (1.0 / (PARTS * WIDTH))
            rstd = lax.rsqrt(var + EPS)
            for p in range(PARTS):
                cols = slice(p * WIDTH, (p + 1) * WIDTH)
                normed[r : r + TILE, cols] = (centred[p] * rstd * gain[:, cols]).astype(BF16)
        here = pl.ds(pl.multiple_of(rows + CAP, CH), CH)
        x = normed[...]
        qk[0, here, :] = (jnp.dot(x, wq[0], preferred_element_type=F32) * QSCALE).astype(BF16)
        qk[1, here, :] = jnp.dot(x, wq[1], preferred_element_type=F32).astype(BF16)
        v = jnp.dot(x, wq[2], preferred_element_type=F32).astype(BF16)
        vv[0, here, 0:128] = v[:, 0:128]
        vv[1, here, 0:128] = v[:, 128:256]

    tail_qk = remote(qk.at[:, pl.ds(ROWS, CAP), :], qk.at[:, pl.ds(0, CAP), :], t_send.at[0], t_recv.at[0], to_after)
    tail_v = remote(
        vv.at[:, pl.ds(ROWS, CAP), pl.ds(0, 128)], vv.at[:, pl.ds(0, CAP), pl.ds(0, 128)],
        t_send.at[1], t_recv.at[1], to_after,
    )

    def arrive(i):
        gather_wait(0, i)
        gather_wait(1, i)
        gather_copy(2, i).start()
        gather_copy(3, i).start()

    def more(i):
        gather_copy(0, i).start()
        gather_copy(1, i).start()

    arrive(0)
    more(AHEAD)

    def gather_step(i, _):
        arrive(i)

        @pl.when(i + AHEAD < NCH)
        def _():
            more(i + AHEAD)

        project(i - 1)

        @pl.when(i == 2)
        def _():
            tail_qk.start()
            tail_v.start()

        return 0

    lax.fori_loop(1, NCH - 1, gather_step, 0)
    arrive(NCH - 1)

    lanes = lax.broadcasted_iota(jnp.int32, (1, 128), 1) < HS

    def attend(block, target):
        first, extent = bands[block]
        rows = slice(block * BLK, (block + 1) * BLK)
        span = slice(first, first + extent)

        def pair_step(pair, _):
            cols = pl.ds(pl.multiple_of(pair * 128, 128), 128)
            q = qk[0, rows, cols]
            for half in range(2):
                q_half = jnp.where(lanes if half == 0 else ~lanes, q, jnp.zeros_like(q))
                for k in range(0, extent, BLK):
                    score[half, :, k : k + BLK] = lax.dot_general(
                        q_half, qk[1, first + k : first + k + BLK, cols], (((1,), (1,)), ((), ())),
                        preferred_element_type=F32,
                    )
            results = []
            for half in range(2):
                for r in range(0, BLK, TILE):
                    allowed = score[half, r : r + TILE, 0:extent] + bias[block * BLK + r : block * BLK + r + TILE, span]
                    top = jnp.max(allowed, axis=1, keepdims=True)
                    prob[half, r : r + TILE, 0:extent] = jnp.exp2(allowed - top).astype(BF16)
                out = jnp.dot(prob[half, :, 0:extent], vv[pair, span, :], preferred_element_type=F32)
                results.append(out[:, 0:128] / out[:, 128:256])
            target[:, cols] = jnp.where(lanes, results[0], results[1]).astype(BF16)
            return 0

        lax.fori_loop(0, 2, pair_step, 0)

    project(NCH - 2)
    project(NCH - 1)
    load_wo.wait()
    give_back = remote(attin, back, b_send, b_recv, to_before)

    half = BLK // 2
    low, high = pl.ds(0, half), pl.ds(half, half)

    def rs_copy(kind, b):
        src, dst, there = (
            (part.at[b, far, low, :], hop.at[b, 0], to_right),
            (part.at[b, far, high, :], hop.at[b, 1], to_left),
            (part.at[b, right, high, :], fin.at[b, 0, high, :], to_right),
            (part.at[b, left, low, :], fin.at[b, 1, low, :], to_left),
            (relay.at[b, 0], fin.at[b, 0, low, :], to_right),
            (relay.at[b, 1], fin.at[b, 1, high, :], to_left),
        )[kind]
        return remote(src, dst, rs_send.at[kind, b], rs_recv.at[kind, b], there)

    def pass_on(b):
        rs_copy(0, b).wait_recv()
        relay[b, 0] = (hop[b, 0].astype(F32) + part[b, right, low, :].astype(F32)).astype(BF16)
        rs_copy(4, b).start()
        rs_copy(1, b).wait_recv()
        relay[b, 1] = (hop[b, 1].astype(F32) + part[b, left, high, :].astype(F32)).astype(BF16)
        rs_copy(5, b).start()

    order = (2, 0, 1, 3)
    for step, b in enumerate(order):
        if step == 1:
            admit()
            tail_qk.wait_recv()
            tail_v.wait_recv()
            attend(0, attin)
            give_back.start()
        attend(b + 1, att)
        if b == NBLK - 1:
            give_back.wait_recv()
            moved = labcol[ALL - BLK : ALL, :] < 0.0
            for cols in (slice(0, 128), slice(128, 256)):
                att[:, cols] = jnp.where(moved, back[:, cols].astype(F32), att[:, cols].astype(F32)).astype(BF16)
        rows = att[...]
        for p in range(PARTS):
            part[b, p] = jnp.dot(
                rows, wo[:, p * WIDTH : (p + 1) * WIDTH], preferred_element_type=F32
            ).astype(BF16)
        for kind in range(4):
            rs_copy(kind, b).start()
        if step >= 1:
            pass_on(order[step - 1])
    pass_on(order[-1])

    def store_out(b):
        rows = pl.ds(b * BLK, BLK)
        return pltpu.make_async_copy(outv.at[rows, :], out_any.at[rows, :], out_sem.at[b])

    def finish(b):
        for kind in range(2, 6):
            rs_copy(kind, b).wait_recv()
        rows = slice(b * BLK, (b + 1) * BLK)
        outv[rows, :] = (
            xg[me, rows, :].astype(F32)
            + part[b, me].astype(F32)
            + fin[b, 0].astype(F32)
            + fin[b, 1].astype(F32)
        ).astype(BF16)

    for b in order:
        finish(b)
        store_out(b).start()

    def drain(i, _):
        for kind in range(4):
            gather_copy(kind, i).wait_send()
        return 0

    lax.fori_loop(0, NCH, drain, 0)
    code.wait_send()
    tail_qk.wait_send()
    tail_v.wait_send()
    give_back.wait_send()
    for b in range(NBLK):
        for kind in range(6):
            rs_copy(kind, b).wait_send()
        store_out(b).wait()


def local(tokens, norm_gain, w_qkv, w_out, window_id, carry):
    there = pl.BlockSpec(memory_space=pltpu.HBM)
    dma = pltpu.SemaphoreType.DMA
    return pl.pallas_call(
        kernel,
        out_shape=jax.ShapeDtypeStruct(tokens.shape, BF16),
        in_specs=[there] * 5 + [pl.BlockSpec(memory_space=pltpu.SMEM)],
        out_specs=pl.BlockSpec(memory_space=pl.ANY),
        scratch_shapes=[
            pltpu.VMEM((1, PARTS * WIDTH), F32),
            pltpu.VMEM((1, ROWS), jnp.int32),
            pltpu.VMEM((PARTS, ROWS, WIDTH), BF16),
            pltpu.VMEM((3, PARTS * WIDTH, WIDTH), BF16),
            pltpu.VMEM((WIDTH, PARTS * WIDTH), BF16),
            pltpu.VMEM((CH, PARTS * WIDTH), BF16),
            pltpu.VMEM((2, ALL, WIDTH), BF16),
            pltpu.VMEM((2, ALL, WIDTH), BF16),
            pltpu.VMEM((8, 128), F32),
            pltpu.VMEM((8, 128), F32),
            pltpu.VMEM((ALL, ALL), F32),
            pltpu.VMEM((ALL, 128), F32),
            pltpu.VMEM((CAP, WIDTH), BF16),
            pltpu.VMEM((BLK, WIDTH), BF16),
            pltpu.VMEM((CAP, WIDTH), BF16),
            pltpu.VMEM((NBLK, PARTS, BLK, WIDTH), BF16),
            pltpu.VMEM((NBLK, 2, BLK // 2, WIDTH), BF16),
            pltpu.VMEM((NBLK, 2, BLK // 2, WIDTH), BF16),
            pltpu.VMEM((NBLK, 2, BLK, WIDTH), BF16),
            pltpu.VMEM((2, BLK, ALL), F32),
            pltpu.VMEM((2, BLK, ALL), BF16),
            pltpu.VMEM((ROWS, WIDTH), BF16),
            dma,
            dma((4,)),
            dma((4, NCH)),
            dma((4, NCH)),
            dma,
            dma,
            dma((2,)),
            dma((2,)),
            dma,
            dma,
            dma((6, NBLK)),
            dma((6, NBLK)),
            dma((NBLK,)),
        ],
        compiler_params=pltpu.CompilerParams(
            collective_id=0, has_side_effects=True, vmem_limit_bytes=56 * 1024 * 1024
        ),
        cost_estimate=pl.CostEstimate(flops=4_000_000_000, bytes_accessed=4_000_000, transcendentals=5_000_000),
    )(tokens, norm_gain.reshape(1, PARTS * WIDTH), w_qkv, w_out, window_id, carry)


def solution(mesh):
    return jax.shard_map(
        local,
        mesh=mesh,
        in_specs=(
            P("space", "head"),
            P(),
            P(None, None, "head"),
            P("head", None),
            P("space", None),
            P("space"),
        ),
        out_specs=P("space", "head"),
        check_vma=False,
    )
```

time: 150 us -> 56.4 us (0.38)
  the two profiles are of different devices: /device:TPU:1 before, /device:TPU:2 now
where the time goes in v1:
time: 56.4 us; the launch traced here: 56.2 us
  Pallas kernels  53.7 us (95%)
  local copies, waits for them, and re-layouts  1.87 us (3%)
  between operations  0.66 us (1%)
    pallas_call x1, Pallas kernels, local(): pl.pallas_call(kernel, out_shape=jax.ShapeDtypeStruct(tokens.shape, BF16)...  53.7 us
    unnamed x1, local copies, waits for them, and re-layouts  1.87 us

profile of v1, /device:TPU:2, one launch (start us, length us, event | category | flops | bytes accessed | tf_op | source)
XLA Modules:
  0.0 56.2 jit_solution(4945960961116710578)
XLA Ops:
  0.7 53.7 %shard_map.64 = bf16[1024,256]{1,0:T(8,128)(2,1)} custom-call(bf16[1024,256]{1,0:T(8,128)(2,1)} %tok_hbm.1, f32[1,1024]{1,0:T(1,128)} %bitcast.1, bf16[3,1024,256]{2,1,0:T(8,128)(2,1)} %wqkv_hbm.1, bf16[256,1024]{1,0:T(8,128)(2,1)} %wout_hbm.1, s32[1,1024]{1,0:T(1,128)} %wid_hbm.1, s32[1]{0:T(128)S(6)} %copy.8.carry_ref), custom_call_target="tpu_custom_call" | custom-call | flops 4000000000 | bytes 4000000 | tf_op jit(solution)/shard_map/pallas_call | solution.py:327
  54.3 1.9 %copy.9 = bf16[1024,256]{1,0:T(8,128)(2,1)} copy(bf16[1024,256]{1,0:T(8,128)(2,1)} %shard_map.64) | data formatting | bytes 1048576

commit v2 on v1

--- a/solution.py
+++ b/solution.py
@@ -30,13 +30,13 @@
 
 
 def chunk_at(i):
-    return (i + NCH - CAP // CH) % NCH
+    return NCH - 2 - 2 * (i // 2) + i % 2
 
 
 def kernel(
     tok_hbm, gain_hbm, wqkv_hbm, wout_hbm, wid_hbm, carry_ref, out_any,
     gain_ref, wid_ref, xg, wq, wo, normed, qk, vv, lab, labin, bias, labcol, back, att, attin, part, hop, relay, fin,
-    score, prob, outv,
+    score, prob, outv, held, top_held, shrink,
     own_sem, wsem, ag_send, ag_recv, c_send, c_recv, t_send, t_recv, b_send, b_recv,
     rs_send, rs_recv, out_sem,
 ):
@@ -202,12 +202,11 @@
         return 0
 
     lax.fori_loop(1, NCH - 1, gather_step, 0)
-    arrive(NCH - 1)
 
     lanes = lax.broadcasted_iota(jnp.int32, (1, 128), 1) < HS
 
-    def attend(block, target):
-        first, extent = bands[block]
+    def attend(block, target, part=None, span=None):
+        first, extent = bands[block] if span is None else span
         rows = slice(block * BLK, (block + 1) * BLK)
         span = slice(first, first + extent)
 
@@ -224,16 +223,34 @@
             results = []
             for half in range(2):
                 for r in range(0, BLK, TILE):
-                    allowed = score[half, r : r + TILE, 0:extent] + bias[block * BLK + r : block * BLK + r + TILE, span]
+                    tile = slice(r, r + TILE)
+                    allowed = score[half, tile, 0:extent] + bias[block * BLK + r : block * BLK + r + TILE, span]
                     top = jnp.max(allowed, axis=1, keepdims=True)
-                    prob[half, r : r + TILE, 0:extent] = jnp.exp2(allowed - top).astype(BF16)
-                out = jnp.dot(prob[half, :, 0:extent], vv[pair, span, :], preferred_element_type=F32)
-                results.append(out[:, 0:128] / out[:, 128:256])
-            target[:, cols] = jnp.where(lanes, results[0], results[1]).astype(BF16)
+                    if part == 0:
+                        top_held[pair, half, tile, :] = jnp.broadcast_to(top, (TILE, 128))
+                    elif part == 1:
+                        old = top_held[pair, half, tile, :]
+                        top = jnp.maximum(old[:, 0:1], top)
+                        shrink[half, tile, :] = jnp.exp2(old - top)
+                    prob[half, tile, 0:extent] = jnp.exp2(allowed - top).astype(BF16)
+                results.append(jnp.dot(prob[half, :, 0:extent], vv[pair, span, :], preferred_element_type=F32))
+            total = jnp.where(lanes, results[0][:, 0:128], results[1][:, 0:128])
+            weight = jnp.where(lanes, results[0][:, 128:256], results[1][:, 128:256])
+            if part == 0:
+                held[pair, 0] = total
+                held[pair, 1] = weight
+            else:
+                if part == 1:
+                    scale = jnp.where(lanes, shrink[0], shrink[1])
+                    total = total + scale * held[pair, 0]
+                    weight = weight + scale * held[pair, 1]
+                target[:, cols] = (total / weight).astype(BF16)
             return 0
 
         lax.fori_loop(0, 2, pair_step, 0)
 
+    attend(3, att, 0, (512, 768))
+    arrive(NCH - 1)
     project(NCH - 2)
     project(NCH - 1)
     load_wo.wait()
@@ -261,16 +278,21 @@
         relay[b, 1] = (hop[b, 1].astype(F32) + part[b, left, high, :].astype(F32)).astype(BF16)
         rs_copy(5, b).start()
 
-    order = (2, 0, 1, 3)
+    order = (2, 1, 0, 3)
     for step, b in enumerate(order):
-        if step == 1:
+        if step == 0:
+            attend(3, att, 1, (256, 256))
+        elif step == 1:
             admit()
             tail_qk.wait_recv()
             tail_v.wait_recv()
+            attend(2, att)
+        elif step == 2:
             attend(0, attin)
             give_back.start()
-        attend(b + 1, att)
-        if b == NBLK - 1:
+            attend(1, att)
+        else:
+            attend(4, att)
             give_back.wait_recv()
             moved = labcol[ALL - BLK : ALL, :] < 0.0
             for cols in (slice(0, 128), slice(128, 256)):
@@ -284,7 +306,6 @@
             rs_copy(kind, b).start()
         if step >= 1:
             pass_on(order[step - 1])
-    pass_on(order[-1])
 
     def store_out(b):
         rows = pl.ds(b * BLK, BLK)
@@ -300,10 +321,13 @@
             + fin[b, 0].astype(F32)
             + fin[b, 1].astype(F32)
         ).astype(BF16)
-
-    for b in order:
-        finish(b)
         store_out(b).start()
+
+    finish(order[0])
+    finish(order[1])
+    pass_on(order[3])
+    finish(order[2])
+    finish(order[3])
 
     def drain(i, _):
         for kind in range(4):
@@ -352,6 +376,9 @@
             pltpu.VMEM((2, BLK, ALL), F32),
             pltpu.VMEM((2, BLK, ALL), BF16),
             pltpu.VMEM((ROWS, WIDTH), BF16),
+            pltpu.VMEM((2, 2, BLK, 128), F32),
+            pltpu.VMEM((2, 2, BLK, 128), F32),
+            pltpu.VMEM((2, BLK, 128), F32),
             dma,
             dma((4,)),
             dma((4, NCH)),

time: 56.4 us -> 57.2 us (1.014)
  the two profiles are of different devices: /device:TPU:2 before, /device:TPU:4 now
where the time goes in v2:
time: 57.2 us; the launch traced here: 57 us
  Pallas kernels  54.5 us (95%)
  local copies, waits for them, and re-layouts  1.87 us (3%)
  between operations  0.66 us (1%)
    pallas_call x1, Pallas kernels, local(): pl.pallas_call(kernel, out_shape=jax.ShapeDtypeStruct(tokens.shape, BF16)...  54.5 us
    unnamed x1, local copies, waits for them, and re-layouts  1.87 us

profile of v2, /device:TPU:4, one launch (start us, length us, event | category | flops | bytes accessed | tf_op | source)
XLA Modules:
  0.0 57.0 jit_solution(4896658440065644536)
XLA Ops:
  0.7 54.5 %shard_map.64 = bf16[1024,256]{1,0:T(8,128)(2,1)} custom-call(bf16[1024,256]{1,0:T(8,128)(2,1)} %tok_hbm.1, f32[1,1024]{1,0:T(1,128)} %bitcast.1, bf16[3,1024,256]{2,1,0:T(8,128)(2,1)} %wqkv_hbm.1, bf16[256,1024]{1,0:T(8,128)(2,1)} %wout_hbm.1, s32[1,1024]{1,0:T(1,128)} %wid_hbm.1, s32[1]{0:T(128)S(6)} %copy.8.carry_ref), custom_call_target="tpu_custom_call" | custom-call | flops 4000000000 | bytes 4000000 | tf_op jit(solution)/shard_map/pallas_call | solution.py:351
  55.2 1.9 %copy.9 = bf16[1024,256]{1,0:T(8,128)(2,1)} copy(bf16[1024,256]{1,0:T(8,128)(2,1)} %shard_map.64) | data formatting | bytes 1048576

commit v3 on v2

--- a/solution.py
+++ b/solution.py
@@ -18,11 +18,12 @@
 ALL = ROWS + CAP
 WIDTH = 256
 PARTS = 4
-CH = 128
+CH = 256
+LANE = 128
 NCH = ROWS // CH
 BLK = 256
 NBLK = ROWS // BLK
-AHEAD = 3
+AHEAD = 2
 TILE = 16
 EPS = 1e-05
 QSCALE = HS**-0.5 * math.log2(math.e)
@@ -30,7 +31,7 @@
 
 
 def chunk_at(i):
-    return NCH - 2 - 2 * (i // 2) + i % 2
+    return NCH - 1 - i
 
 
 def kernel(
@@ -103,19 +104,19 @@
     code = remote(lab, labin, c_send, c_recv, to_after)
     code.start()
 
-    vv[:, :, CH:] = jnp.ones((2, ALL, CH), BF16)
+    vv[:, :, LANE:] = jnp.ones((2, ALL, LANE), BF16)
 
     def columns_of(queries, first):
-        for k in range(queries.shape[1] // CH):
-            piece = jnp.broadcast_to(queries[0:1, k * CH : (k + 1) * CH], (CH, CH))
-            labcol[first + k * CH : first + (k + 1) * CH, :] = piece.T
+        for k in range(queries.shape[1] // LANE):
+            piece = jnp.broadcast_to(queries[0:1, k * LANE : (k + 1) * LANE], (LANE, LANE))
+            labcol[first + k * LANE : first + (k + 1) * LANE, :] = piece.T
 
     def allow(block, queries, first, start, stop):
         keys = jnp.where(queries < 0.0, -2.0, queries)
         rows = slice(block * BLK, (block + 1) * BLK)
         column = labcol[rows, :]
-        for k in range(start, stop, CH):
-            bias[rows, k : k + CH] = jnp.where(column == keys[0:1, k - first : k - first + CH], 0.0, NEG)
+        for k in range(start, stop, LANE):
+            bias[rows, k : k + LANE] = jnp.where(column == keys[0:1, k - first : k - first + LANE], 0.0, NEG)
 
     def labels_here():
         spread = jnp.broadcast_to(wid_ref[...].astype(F32), (8, ROWS))
@@ -183,25 +184,15 @@
         gather_copy(1, i).start()
 
     arrive(0)
-    more(AHEAD)
-
-    def gather_step(i, _):
-        arrive(i)
-
-        @pl.when(i + AHEAD < NCH)
-        def _():
-            more(i + AHEAD)
-
-        project(i - 1)
-
-        @pl.when(i == 2)
-        def _():
-            tail_qk.start()
-            tail_v.start()
-
-        return 0
-
-    lax.fori_loop(1, NCH - 1, gather_step, 0)
+    more(2)
+    arrive(1)
+    more(3)
+    project(0)
+    tail_qk.start()
+    tail_v.start()
+    arrive(2)
+    project(1)
+    arrive(3)
 
     lanes = lax.broadcasted_iota(jnp.int32, (1, 128), 1) < HS
 
@@ -249,10 +240,9 @@
 
         lax.fori_loop(0, 2, pair_step, 0)
 
+    project(2)
     attend(3, att, 0, (512, 768))
-    arrive(NCH - 1)
-    project(NCH - 2)
-    project(NCH - 1)
+    project(3)
     load_wo.wait()
     give_back = remote(attin, back, b_send, b_recv, to_before)
 
@@ -345,10 +335,21 @@
         store_out(b).wait()
 
 
+def write_out(src, dst, sem):
+    pieces = [
+        pltpu.make_async_copy(src.at[pl.ds(b * BLK, BLK), :], dst.at[pl.ds(b * BLK, BLK), :], sem.at[b])
+        for b in range(NBLK)
+    ]
+    for piece in pieces:
+        piece.start()
+    for piece in pieces:
+        piece.wait()
+
+
 def local(tokens, norm_gain, w_qkv, w_out, window_id, carry):
     there = pl.BlockSpec(memory_space=pltpu.HBM)
     dma = pltpu.SemaphoreType.DMA
-    return pl.pallas_call(
+    result = pl.pallas_call(
         kernel,
         out_shape=jax.ShapeDtypeStruct(tokens.shape, BF16),
         in_specs=[there] * 5 + [pl.BlockSpec(memory_space=pltpu.SMEM)],
@@ -398,6 +399,15 @@
         ),
         cost_estimate=pl.CostEstimate(flops=4_000_000_000, bytes_accessed=4_000_000, transcendentals=5_000_000),
     )(tokens, norm_gain.reshape(1, PARTS * WIDTH), w_qkv, w_out, window_id, carry)
+    anywhere = pl.BlockSpec(memory_space=pl.ANY)
+    return pl.pallas_call(
+        write_out,
+        out_shape=jax.ShapeDtypeStruct(tokens.shape, BF16),
+        in_specs=[anywhere],
+        out_specs=anywhere,
+        scratch_shapes=[dma((NBLK,))],
+        compiler_params=pltpu.CompilerParams(vmem_limit_bytes=60 * 1024 * 1024),
+    )(result)
 
 
 def solution(mesh):

time: 57.2 us -> 68.5 us (1.20)
  the two profiles are of different devices: /device:TPU:4 before, /device:TPU:2 now
where the time goes in v3:
time: 68.5 us; the launch traced here: 68.4 us
  Pallas kernels  67.7 us (99%)
    pallas_call x1, Pallas kernels, local(): pl.pallas_call(kernel, out_shape=jax.ShapeDtypeStruct(tokens.shape, BF16)...  50.7 us
    pallas_call x1, Pallas kernels, local(): pl.pallas_call(write_out, out_shape=jax.ShapeDtypeStruct(tokens.shape, BF...  17 us

profile of v3, /device:TPU:2, one launch (start us, length us, event | category | flops | bytes accessed | tf_op | source)
XLA Modules:
  0.0 68.4 jit_solution(7408687233954023371)
XLA Ops:
  0.7 50.7 %shard_map.64.src = bf16[1024,256]{1,0:T(8,128)(2,1)} custom-call(bf16[1024,256]{1,0:T(8,128)(2,1)} %tok_hbm.1, f32[1,1024]{1,0:T(1,128)} %bitcast.1, bf16[3,1024,256]{2,1,0:T(8,128)(2,1)} %wqkv_hbm.1, bf16[256,1024]{1,0:T(8,128)(2,1)} %wout_hbm.1, s32[1,1024]{1,0:T(1,128)} %wid_hbm.1, s32[1]{0:T(128)S(6)} %copy.7.carry_ref), custom_call_target="tpu_custom_call" | custom-call | flops 4000000000 | bytes 4000000 | tf_op jit(solution)/shard_map/pallas_call | solution.py:352
  51.3 17.0 %shard_map.65 = bf16[1024,256]{1,0:T(8,128)(2,1)} custom-call(bf16[1024,256]{1,0:T(8,128)(2,1)} %shard_map.64.src), custom_call_target="tpu_custom_call" | custom-call | tf_op jit(solution)/shard_map/pallas_call | solution.py:403

commit v4 on v3

--- a/solution.py
+++ b/solution.py
@@ -36,7 +36,7 @@
 
 def kernel(
     tok_hbm, gain_hbm, wqkv_hbm, wout_hbm, wid_hbm, carry_ref, out_any,
-    gain_ref, wid_ref, xg, wq, wo, normed, qk, vv, lab, labin, bias, labcol, back, att, attin, part, hop, relay, fin,
+    gain_ref, wid_ref, xg, wq, wo, normed, qq, kt, vv, lab, labin, bias, labcol, back, att, attin, part, hop, relay, fin,
     score, prob, outv, held, top_held, shrink,
     own_sem, wsem, ag_send, ag_recv, c_send, c_recv, t_send, t_recv, b_send, b_recv,
     rs_send, rs_recv, out_sem,
@@ -147,10 +147,10 @@
     def project(i):
         gather_wait(2, i)
         gather_wait(3, i)
-        rows = pl.multiple_of(chunk_at(i) * CH, CH)
+        rows = chunk_at(i) * CH
         for r in range(0, CH, TILE):
             slices = [
-                xg[p, pl.ds(pl.multiple_of(rows + r, TILE), TILE), :].astype(F32) for p in range(PARTS)
+                xg[p, rows + r : rows + r + TILE, :].astype(F32) for p in range(PARTS)
             ]
             mean = jnp.sum(sum(slices), axis=1, keepdims=True) * (1.0 / (PARTS * WIDTH))
             centred = [x - mean for x in slices]
@@ -159,15 +159,16 @@
             for p in range(PARTS):
                 cols = slice(p * WIDTH, (p + 1) * WIDTH)
                 normed[r : r + TILE, cols] = (centred[p] * rstd * gain[:, cols]).astype(BF16)
-        here = pl.ds(pl.multiple_of(rows + CAP, CH), CH)
+        here = pl.ds(rows + CAP, CH)
         x = normed[...]
-        qk[0, here, :] = (jnp.dot(x, wq[0], preferred_element_type=F32) * QSCALE).astype(BF16)
-        qk[1, here, :] = jnp.dot(x, wq[1], preferred_element_type=F32).astype(BF16)
+        qq[here, :] = (jnp.dot(x, wq[0], preferred_element_type=F32) * QSCALE).astype(BF16)
+        kt[:, here] = jnp.dot(x, wq[1], preferred_element_type=F32).T.astype(BF16)
         v = jnp.dot(x, wq[2], preferred_element_type=F32).astype(BF16)
         vv[0, here, 0:128] = v[:, 0:128]
         vv[1, here, 0:128] = v[:, 128:256]
 
-    tail_qk = remote(qk.at[:, pl.ds(ROWS, CAP), :], qk.at[:, pl.ds(0, CAP), :], t_send.at[0], t_recv.at[0], to_after)
+    tail_q = remote(qq.at[pl.ds(ROWS, CAP), :], qq.at[pl.ds(0, CAP), :], t_send.at[0], t_recv.at[0], to_after)
+    tail_k = remote(kt.at[:, pl.ds(ROWS, CAP)], kt.at[:, pl.ds(0, CAP)], t_send.at[2], t_recv.at[2], to_after)
     tail_v = remote(
         vv.at[:, pl.ds(ROWS, CAP), pl.ds(0, 128)], vv.at[:, pl.ds(0, CAP), pl.ds(0, 128)],
         t_send.at[1], t_recv.at[1], to_after,
@@ -188,7 +189,8 @@
     arrive(1)
     more(3)
     project(0)
-    tail_qk.start()
+    tail_q.start()
+    tail_k.start()
     tail_v.start()
     arrive(2)
     project(1)
@@ -203,13 +205,12 @@
 
         def pair_step(pair, _):
             cols = pl.ds(pl.multiple_of(pair * 128, 128), 128)
-            q = qk[0, rows, cols]
+            q = qq[rows, cols]
             for half in range(2):
                 q_half = jnp.where(lanes if half == 0 else ~lanes, q, jnp.zeros_like(q))
                 for k in range(0, extent, BLK):
-                    score[half, :, k : k + BLK] = lax.dot_general(
-                        q_half, qk[1, first + k : first + k + BLK, cols], (((1,), (1,)), ((), ())),
-                        preferred_element_type=F32,
+                    score[half, :, k : k + BLK] = jnp.dot(
+                        q_half, kt[cols, first + k : first + k + BLK], preferred_element_type=F32
                     )
             results = []
             for half in range(2):
@@ -274,15 +275,18 @@
             attend(3, att, 1, (256, 256))
         elif step == 1:
             admit()
-            tail_qk.wait_recv()
+            tail_q.wait_recv()
+            tail_k.wait_recv()
             tail_v.wait_recv()
             attend(2, att)
         elif step == 2:
             attend(0, attin)
             give_back.start()
+            pass_on(order[1])
             attend(1, att)
         else:
             attend(4, att)
+            pass_on(order[2])
             give_back.wait_recv()
             moved = labcol[ALL - BLK : ALL, :] < 0.0
             for cols in (slice(0, 128), slice(128, 256)):
@@ -294,8 +298,8 @@
             ).astype(BF16)
         for kind in range(4):
             rs_copy(kind, b).start()
-        if step >= 1:
-            pass_on(order[step - 1])
+        if step == 1:
+            pass_on(order[0])
 
     def store_out(b):
         rows = pl.ds(b * BLK, BLK)
@@ -326,7 +330,8 @@
 
     lax.fori_loop(0, NCH, drain, 0)
     code.wait_send()
-    tail_qk.wait_send()
+    tail_q.wait_send()
+    tail_k.wait_send()
     tail_v.wait_send()
     give_back.wait_send()
     for b in range(NBLK):
@@ -335,21 +340,10 @@
         store_out(b).wait()
 
 
-def write_out(src, dst, sem):
-    pieces = [
-        pltpu.make_async_copy(src.at[pl.ds(b * BLK, BLK), :], dst.at[pl.ds(b * BLK, BLK), :], sem.at[b])
-        for b in range(NBLK)
-    ]
-    for piece in pieces:
-        piece.start()
-    for piece in pieces:
-        piece.wait()
-
-
 def local(tokens, norm_gain, w_qkv, w_out, window_id, carry):
     there = pl.BlockSpec(memory_space=pltpu.HBM)
     dma = pltpu.SemaphoreType.DMA
-    result = pl.pallas_call(
+    return pl.pallas_call(
         kernel,
         out_shape=jax.ShapeDtypeStruct(tokens.shape, BF16),
         in_specs=[there] * 5 + [pl.BlockSpec(memory_space=pltpu.SMEM)],
@@ -361,7 +355,8 @@
             pltpu.VMEM((3, PARTS * WIDTH, WIDTH), BF16),
             pltpu.VMEM((WIDTH, PARTS * WIDTH), BF16),
             pltpu.VMEM((CH, PARTS * WIDTH), BF16),
-            pltpu.VMEM((2, ALL, WIDTH), BF16),
+            pltpu.VMEM((ALL, WIDTH), BF16),
+            pltpu.VMEM((WIDTH, ALL), BF16),
             pltpu.VMEM((2, ALL, WIDTH), BF16),
             pltpu.VMEM((8, 128), F32),
             pltpu.VMEM((8, 128), F32),
@@ -386,8 +381,8 @@
             dma((4, NCH)),
             dma,
             dma,
-            dma((2,)),
-            dma((2,)),
+            dma((3,)),
+            dma((3,)),
             dma,
             dma,
             dma((6, NBLK)),
@@ -399,15 +394,6 @@
         ),
         cost_estimate=pl.CostEstimate(flops=4_000_000_000, bytes_accessed=4_000_000, transcendentals=5_000_000),
     )(tokens, norm_gain.reshape(1, PARTS * WIDTH), w_qkv, w_out, window_id, carry)
-    anywhere = pl.BlockSpec(memory_space=pl.ANY)
-    return pl.pallas_call(
-        write_out,
-        out_shape=jax.ShapeDtypeStruct(tokens.shape, BF16),
-        in_specs=[anywhere],
-        out_specs=anywhere,
-        scratch_shapes=[dma((NBLK,))],
-        compiler_params=pltpu.CompilerParams(vmem_limit_bytes=60 * 1024 * 1024),
-    )(result)
 
 
 def solution(mesh):

time: 68.5 us -> 55.5 us (0.81)
  Pallas kernels: 67.7 us -> 52.8 us
  local copies, waits for them, and re-layouts: 0 us -> 1.87 us
    pallas_call x1 -> x0, Pallas kernels: 17 us -> none  [local(): pl.pallas_call(write_out, out_shape=jax.ShapeDtypeStruct(tokens.shape, BF...]
    pallas_call x1, Pallas kernels: 50.7 us -> 52.8 us  [local(): pl.pallas_call(kernel, out_shape=jax.ShapeDtypeStruct(tokens.shape, BF16)...]
    unnamed x0 -> x1, local copies, waits for them, and re-layouts: none -> 1.87 us
where the time goes in v4:
time: 55.5 us; the launch traced here: 55.3 us
  Pallas kernels  52.8 us (95%)
  local copies, waits for them, and re-layouts  1.87 us (3%)
  between operations  0.66 us (1%)
    pallas_call x1, Pallas kernels, local(): pl.pallas_call(kernel, out_shape=jax.ShapeDtypeStruct(tokens.shape, BF16)...  52.8 us
    unnamed x1, local copies, waits for them, and re-layouts  1.87 us

profile of v4, /device:TPU:2, one launch (start us, length us, event | category | flops | bytes accessed | tf_op | source)
XLA Modules:
  0.0 55.3 jit_solution(5832682336903170028)
XLA Ops:
  0.7 52.8 %shard_map.64 = bf16[1024,256]{1,0:T(8,128)(2,1)} custom-call(bf16[1024,256]{1,0:T(8,128)(2,1)} %tok_hbm.1, f32[1,1024]{1,0:T(1,128)} %bitcast.1, bf16[3,1024,256]{2,1,0:T(8,128)(2,1)} %wqkv_hbm.1, bf16[256,1024]{1,0:T(8,128)(2,1)} %wout_hbm.1, s32[1,1024]{1,0:T(1,128)} %wid_hbm.1, s32[1]{0:T(128)S(6)} %copy.8.carry_ref), custom_call_target="tpu_custom_call" | custom-call | flops 4000000000 | bytes 4000000 | tf_op jit(solution)/shard_map/pallas_call | solution.py:346
  53.5 1.9 %copy.9 = bf16[1024,256]{1,0:T(8,128)(2,1)} copy(bf16[1024,256]{1,0:T(8,128)(2,1)} %shard_map.64) | data formatting | bytes 1048576

commit v5 on v3

--- a/solution.py
+++ b/solution.py
@@ -314,8 +314,8 @@
         store_out(b).start()
 
     finish(order[0])
+    pass_on(order[3])
     finish(order[1])
-    pass_on(order[3])
     finish(order[2])
     finish(order[3])
 
@@ -335,21 +335,10 @@
         store_out(b).wait()
 
 
-def write_out(src, dst, sem):
-    pieces = [
-        pltpu.make_async_copy(src.at[pl.ds(b * BLK, BLK), :], dst.at[pl.ds(b * BLK, BLK), :], sem.at[b])
-        for b in range(NBLK)
-    ]
-    for piece in pieces:
-        piece.start()
-    for piece in pieces:
-        piece.wait()
-
-
 def local(tokens, norm_gain, w_qkv, w_out, window_id, carry):
     there = pl.BlockSpec(memory_space=pltpu.HBM)
     dma = pltpu.SemaphoreType.DMA
-    result = pl.pallas_call(
+    return pl.pallas_call(
         kernel,
         out_shape=jax.ShapeDtypeStruct(tokens.shape, BF16),
         in_specs=[there] * 5 + [pl.BlockSpec(memory_space=pltpu.SMEM)],
@@ -399,15 +388,6 @@
         ),
         cost_estimate=pl.CostEstimate(flops=4_000_000_000, bytes_accessed=4_000_000, transcendentals=5_000_000),
     )(tokens, norm_gain.reshape(1, PARTS * WIDTH), w_qkv, w_out, window_id, carry)
-    anywhere = pl.BlockSpec(memory_space=pl.ANY)
-    return pl.pallas_call(
-        write_out,
-        out_shape=jax.ShapeDtypeStruct(tokens.shape, BF16),
-        in_specs=[anywhere],
-        out_specs=anywhere,
-        scratch_shapes=[dma((NBLK,))],
-        compiler_params=pltpu.CompilerParams(vmem_limit_bytes=60 * 1024 * 1024),
-    )(result)
 
 
 def solution(mesh):

time: 68.5 us -> 53.4 us (0.78)
  Pallas kernels: 67.7 us -> 50.7 us
  local copies, waits for them, and re-layouts: 0 us -> 1.87 us
    pallas_call x1 -> x0, Pallas kernels: 17 us -> none  [local(): pl.pallas_call(write_out, out_shape=jax.ShapeDtypeStruct(tokens.shape, BF...]
    unnamed x0 -> x1, local copies, waits for them, and re-layouts: none -> 1.87 us
where the time goes in v5:
time: 53.4 us; the launch traced here: 53.2 us
  Pallas kernels  50.7 us (95%)
  local copies, waits for them, and re-layouts  1.87 us (4%)
  between operations  0.66 us (1%)
    pallas_call x1, Pallas kernels, local(): pl.pallas_call(kernel, out_shape=jax.ShapeDtypeStruct(tokens.shape, BF16)...  50.7 us
    unnamed x1, local copies, waits for them, and re-layouts  1.87 us

profile of v5, /device:TPU:2, one launch (start us, length us, event | category | flops | bytes accessed | tf_op | source)
XLA Modules:
  0.0 53.2 jit_solution(5693705192453899149)
XLA Ops:
  0.7 50.7 %shard_map.64 = bf16[1024,256]{1,0:T(8,128)(2,1)} custom-call(bf16[1024,256]{1,0:T(8,128)(2,1)} %tok_hbm.1, f32[1,1024]{1,0:T(1,128)} %bitcast.1, bf16[3,1024,256]{2,1,0:T(8,128)(2,1)} %wqkv_hbm.1, bf16[256,1024]{1,0:T(8,128)(2,1)} %wout_hbm.1, s32[1,1024]{1,0:T(1,128)} %wid_hbm.1, s32[1]{0:T(128)S(6)} %copy.8.carry_ref), custom_call_target="tpu_custom_call" | custom-call | flops 4000000000 | bytes 4000000 | tf_op jit(solution)/shard_map/pallas_call | solution.py:341
  51.3 1.9 %copy.9 = bf16[1024,256]{1,0:T(8,128)(2,1)} copy(bf16[1024,256]{1,0:T(8,128)(2,1)} %shard_map.64) | data formatting | bytes 1048576

commit v6 on v5

--- a/solution.py
+++ b/solution.py
@@ -192,7 +192,6 @@
     tail_v.start()
     arrive(2)
     project(1)
-    arrive(3)
 
     lanes = lax.broadcasted_iota(jnp.int32, (1, 128), 1) < HS
 
@@ -240,8 +239,9 @@
 
         lax.fori_loop(0, 2, pair_step, 0)
 
+    attend(3, att, 0, (768, 512))
+    arrive(3)
     project(2)
-    attend(3, att, 0, (512, 768))
     project(3)
     load_wo.wait()
     give_back = remote(attin, back, b_send, b_recv, to_before)
@@ -271,7 +271,7 @@
     order = (2, 1, 0, 3)
     for step, b in enumerate(order):
         if step == 0:
-            attend(3, att, 1, (256, 256))
+            attend(3, att, 1, (256, 512))
         elif step == 1:
             admit()
             tail_qk.wait_recv()
@@ -294,8 +294,8 @@
             ).astype(BF16)
         for kind in range(4):
             rs_copy(kind, b).start()
-        if step >= 1:
-            pass_on(order[step - 1])
+        if step >= 2:
+            pass_on(order[step - 2])
 
     def store_out(b):
         rows = pl.ds(b * BLK, BLK)
@@ -313,6 +313,7 @@
         ).astype(BF16)
         store_out(b).start()
 
+    pass_on(order[2])
     finish(order[0])
     pass_on(order[3])
     finish(order[1])

time: 53.4 us -> 54.4 us (1.019)
  Pallas kernels: 50.7 us -> 51.6 us
    pallas_call x1, Pallas kernels: 50.7 us -> 51.6 us  [local(): pl.pallas_call(kernel, out_shape=jax.ShapeDtypeStruct(tokens.shape, BF16)...]
where the time goes in v6:
time: 54.4 us; the launch traced here: 54.2 us
  Pallas kernels  51.6 us (95%)
  local copies, waits for them, and re-layouts  1.87 us (3%)
  between operations  0.66 us (1%)
    pallas_call x1, Pallas kernels, local(): pl.pallas_call(kernel, out_shape=jax.ShapeDtypeStruct(tokens.shape, BF16)...  51.6 us
    unnamed x1, local copies, waits for them, and re-layouts  1.87 us

profile of v6, /device:TPU:2, one launch (start us, length us, event | category | flops | bytes accessed | tf_op | source)
XLA Modules:
  0.0 54.2 jit_solution(10743467717170332351)
XLA Ops:
  0.7 51.6 %shard_map.64 = bf16[1024,256]{1,0:T(8,128)(2,1)} custom-call(bf16[1024,256]{1,0:T(8,128)(2,1)} %tok_hbm.1, f32[1,1024]{1,0:T(1,128)} %bitcast.1, bf16[3,1024,256]{2,1,0:T(8,128)(2,1)} %wqkv_hbm.1, bf16[256,1024]{1,0:T(8,128)(2,1)} %wout_hbm.1, s32[1,1024]{1,0:T(1,128)} %wid_hbm.1, s32[1]{0:T(128)S(6)} %copy.8.carry_ref), custom_call_target="tpu_custom_call" | custom-call | flops 4000000000 | bytes 4000000 | tf_op jit(solution)/shard_map/pallas_call | solution.py:342
  52.3 1.9 %copy.9 = bf16[1024,256]{1,0:T(8,128)(2,1)} copy(bf16[1024,256]{1,0:T(8,128)(2,1)} %shard_map.64) | data formatting | bytes 1048576

commit v7 on v6

--- a/solution.py
+++ b/solution.py
@@ -280,9 +280,11 @@
         elif step == 2:
             attend(0, attin)
             give_back.start()
+            pass_on(order[1])
             attend(1, att)
         else:
             attend(4, att)
+            pass_on(order[2])
             give_back.wait_recv()
             moved = labcol[ALL - BLK : ALL, :] < 0.0
             for cols in (slice(0, 128), slice(128, 256)):
@@ -294,8 +296,8 @@
             ).astype(BF16)
         for kind in range(4):
             rs_copy(kind, b).start()
-        if step >= 2:
-            pass_on(order[step - 2])
+        if step == 1:
+            pass_on(order[0])
 
     def store_out(b):
         rows = pl.ds(b * BLK, BLK)
@@ -313,7 +315,6 @@
         ).astype(BF16)
         store_out(b).start()
 
-    pass_on(order[2])
     finish(order[0])
     pass_on(order[3])
     finish(order[1])

time: 54.4 us -> 56.7 us (1.042)
  Pallas kernels: 51.6 us -> 54 us
    pallas_call x1, Pallas kernels: 51.6 us -> 54 us  [local(): pl.pallas_call(kernel, out_shape=jax.ShapeDtypeStruct(tokens.shape, BF16)...]
where the time goes in v7:
time: 56.7 us; the launch traced here: 56.5 us
  Pallas kernels  54 us (95%)
  local copies, waits for them, and re-layouts  1.87 us (3%)
  between operations  0.66 us (1%)
    pallas_call x1, Pallas kernels, local(): pl.pallas_call(kernel, out_shape=jax.ShapeDtypeStruct(tokens.shape, BF16)...  54 us
    unnamed x1, local copies, waits for them, and re-layouts  1.87 us

profile of v7, /device:TPU:2, one launch (start us, length us, event | category | flops | bytes accessed | tf_op | source)
XLA Modules:
  0.0 56.5 jit_solution(16219685529348693236)
XLA Ops:
  0.7 54.0 %shard_map.64 = bf16[1024,256]{1,0:T(8,128)(2,1)} custom-call(bf16[1024,256]{1,0:T(8,128)(2,1)} %tok_hbm.1, f32[1,1024]{1,0:T(1,128)} %bitcast.1, bf16[3,1024,256]{2,1,0:T(8,128)(2,1)} %wqkv_hbm.1, bf16[256,1024]{1,0:T(8,128)(2,1)} %wout_hbm.1, s32[1,1024]{1,0:T(1,128)} %wid_hbm.1, s32[1]{0:T(128)S(6)} %copy.8.carry_ref), custom_call_target="tpu_custom_call" | custom-call | flops 4000000000 | bytes 4000000 | tf_op jit(solution)/shard_map/pallas_call | solution.py:343
  54.6 1.9 %copy.9 = bf16[1024,256]{1,0:T(8,128)(2,1)} copy(bf16[1024,256]{1,0:T(8,128)(2,1)} %shard_map.64) | data formatting | bytes 1048576

commit v8 on v5

--- a/solution.py
+++ b/solution.py
@@ -292,10 +292,12 @@
             part[b, p] = jnp.dot(
                 rows, wo[:, p * WIDTH : (p + 1) * WIDTH], preferred_element_type=F32
             ).astype(BF16)
-        for kind in range(4):
+        for kind in (0, 1):
             rs_copy(kind, b).start()
         if step >= 1:
             pass_on(order[step - 1])
+        for kind in (2, 3):
+            rs_copy(kind, b).start()
 
     def store_out(b):
         rows = pl.ds(b * BLK, BLK)

time: 53.4 us -> 53.4 us (level)
  no operation moved by 1% of the time
where the time goes in v8:
time: 53.4 us; the launch traced here: 53.2 us
  Pallas kernels  50.7 us (95%)
  local copies, waits for them, and re-layouts  1.87 us (4%)
  between operations  0.66 us (1%)
    pallas_call x1, Pallas kernels, local(): pl.pallas_call(kernel, out_shape=jax.ShapeDtypeStruct(tokens.shape, BF16)...  50.7 us
    unnamed x1, local copies, waits for them, and re-layouts  1.87 us

profile of v8, /device:TPU:2, one launch (start us, length us, event | category | flops | bytes accessed | tf_op | source)
XLA Modules:
  0.0 53.2 jit_solution(13924534246655881900)
XLA Ops:
  0.7 50.7 %shard_map.64 = bf16[1024,256]{1,0:T(8,128)(2,1)} custom-call(bf16[1024,256]{1,0:T(8,128)(2,1)} %tok_hbm.1, f32[1,1024]{1,0:T(1,128)} %bitcast.1, bf16[3,1024,256]{2,1,0:T(8,128)(2,1)} %wqkv_hbm.1, bf16[256,1024]{1,0:T(8,128)(2,1)} %wout_hbm.1, s32[1,1024]{1,0:T(1,128)} %wid_hbm.1, s32[1]{0:T(128)S(6)} %copy.8.carry_ref), custom_call_target="tpu_custom_call" | custom-call | flops 4000000000 | bytes 4000000 | tf_op jit(solution)/shard_map/pallas_call | solution.py:343
  51.4 1.9 %copy.9 = bf16[1024,256]{1,0:T(8,128)(2,1)} copy(bf16[1024,256]{1,0:T(8,128)(2,1)} %shard_map.64) | data formatting | bytes 1048576
